TPU v7x, 256 devices: a whole 4x4x8 slice. The times are simulated.
256 devices in a mesh: vid: 16 (over y_hi, z), seq: 16 (over x, y_lo, core).
Axes of the slice: x: 4, y: 4 (y_hi: 2, y_lo: 2; y = y_hi * 2 + y_lo), z: 8, core: 2. Of those that a mesh axis runs over, the one named last changes fastest.
Arguments:
- video: bfloat16 [16, 512, 4096], P('vid', 'seq'), may hold values from -8 to 8
- video_length: int32 [16], P('vid'), may hold values from 128 to 512
- prompt: bfloat16 [16, 128, 4096], P('vid', 'seq'), may hold values from -6 to 6
- prompt_length: int32 [16], replicated, may hold values from 32 to 128
- prompt_choice: int32 [16], P('vid'), may hold values from 0 to 15
- ffn_gain: float32 [4096], replicated, may hold values from 0.1 to 1.9
- ffn_gate: bfloat16 [4096, 6144], P(None, 'seq'), may hold values from -0.09375 to 0.09375
- ffn_up: bfloat16 [4096, 6144], P(None, 'seq'), may hold values from -0.09375 to 0.09375
- ffn_down: bfloat16 [6144, 4096], P('seq'), may hold values from -0.078125 to 0.078125
- final_gain: float32 [4096], replicated, may hold values from 0.1 to 1.9
- video_gain: float32 [4096], replicated, may hold values from 0.1 to 1.9
- w_query: bfloat16 [4096, 4096], P('vid', 'seq'), may hold values from -1 to 1
- w_key: bfloat16 [4096, 4096], P('vid', 'seq'), may hold values from -3 to 3
- w_value: bfloat16 [4096, 4096], P('vid', 'seq'), may hold values from -0.09375 to 0.09375
- w_text_key: bfloat16 [4096, 4096], P('vid', 'seq'), may hold values from -0.09375 to 0.09375
- w_text_value: bfloat16 [4096, 4096], P('vid', 'seq'), may hold values from -0.09375 to 0.09375
- w_out: bfloat16 [4096, 4096], P('seq', 'vid'), may hold values from -0.09375 to 0.09375
Outputs:
- updated: bfloat16 [16, 512, 4096], P('vid', 'seq')
Inputs may be any that keep to these rules, and one draw needn't show every extreme that they name: `prompt_choice`: A prompt may serve several videos or none.
All inputs are finite; a program needn't handle non-finite values.
Results may differ from a plain program's by a relative error of at most 0.0085.
Values may be sent and summed in bfloat16 or wider, within the bound.
A program may use at most 128 MiB of HBM per device.

v0:
```python
import jax
import jax.numpy as jnp
from jax import lax
from jax.sharding import PartitionSpec as P

HD = 128
epsilon = 1e-06


def sent_to_all(x, axis):
    devices = lax.axis_size(axis)
    return lax.all_to_all(jnp.broadcast_to(x[None], (devices, *x.shape)), axis, 0, 0, tiled=True)


def laid_out(tiles, dim):
    lengths = list(tiles.shape[1:])
    lengths[dim] *= tiles.shape[0]
    return jnp.moveaxis(tiles, 0, dim).reshape(lengths)


def gathered_copies(x, axis, dim):
    tiles = sent_to_all(x, axis)
    return laid_out(tiles, dim)


def in_blocks(x, dim, devices):
    lengths = x.shape
    tiles = x.reshape(*lengths[:dim], devices, lengths[dim] // devices, *lengths[dim + 1 :])
    return jnp.moveaxis(tiles, dim, 0)


def sent_and_summed(x, axis, dim):
    tiles = in_blocks(x, dim, lax.axis_size(axis))
    arrived = lax.all_to_all(tiles, axis, split_axis=0, concat_axis=0, tiled=True)
    return arrived.astype(jnp.float32).sum(axis=0)


def side_by_side(arrays, axis, dim, along):
    both = jnp.concatenate(arrays, axis=along)
    whole, at, finished = (lax.all_gather(both, axis, axis=dim, tiled=True), 0, [])
    for a in arrays:
        finished.append(lax.slice_in_dim(whole, at, at + a.shape[along], axis=along))
        at += a.shape[along]
    return tuple(finished)


def rms_norm(values, gain):
    return values * lax.rsqrt(jnp.mean(values * values, axis=-1, keepdims=True) + epsilon) * gain


def prompt_path(
    prompt,
    prompt_length,
    prompt_choice,
    ffn_gain,
    ffn_gate,
    ffn_up,
    ffn_down,
    final_gain,
    w_text_key,
    w_text_value,
):
    gathered = gathered_copies(prompt, "seq", 1)[0]
    residual = gathered.astype(jnp.float32)
    ffn_normed = rms_norm(residual, ffn_gain).astype(jnp.bfloat16)
    gate_proj = jnp.dot(ffn_normed, ffn_gate, preferred_element_type=jnp.float32)
    up_proj = jnp.dot(ffn_normed, ffn_up, preferred_element_type=jnp.float32)
    ffn_hidden = (jax.nn.gelu(gate_proj, approximate=True) * up_proj).astype(jnp.bfloat16)
    partial_value = jnp.dot(ffn_hidden, ffn_down, preferred_element_type=jnp.float32)
    share = sent_and_summed(partial_value.astype(jnp.bfloat16), "seq", 0)
    own_rows = prompt[0].astype(jnp.float32)
    text_share = rms_norm(own_rows + share, final_gain).astype(jnp.bfloat16)
    text = gathered_copies(text_share, "seq", 0)
    blocks = side_by_side((w_text_key, w_text_value), "vid", 0, 1)
    key_sum = jnp.dot(text, blocks[0], preferred_element_type=jnp.float32)
    value_sum = jnp.dot(text, blocks[1], preferred_element_type=jnp.float32)
    text_key = key_sum.astype(jnp.bfloat16)[None]
    text_value = value_sum.astype(jnp.bfloat16)[None]
    wanted = prompt_choice[0]
    blocks = side_by_side((text_key, text_value), "vid", 0, 1)
    number = blocks[0].shape[0]
    chosen = jnp.arange(number, dtype=jnp.int32) == wanted
    picked_key = jnp.sum(
        jnp.where(chosen[:, None, None], blocks[0], jnp.zeros_like(blocks[0])), axis=0
    )
    picked_value = jnp.sum(
        jnp.where(chosen[:, None, None], blocks[1], jnp.zeros_like(blocks[1])), axis=0
    )
    prompt_ids = jnp.arange(prompt_length.shape[0], dtype=jnp.int32)
    text_live = jnp.sum(jnp.where(prompt_ids == wanted, prompt_length, 0))
    return (picked_key, picked_value, text_live)


def video_path(residual, video_gain, w_query, w_key, w_value):
    normed = rms_norm(residual, video_gain).astype(jnp.bfloat16)
    whole_rows = lax.all_gather(normed, "seq", axis=0, tiled=True)
    blocks = side_by_side((w_query, w_key, w_value), "vid", 0, 1)
    query_sum, key_sum, value_sum = tuple(
        (
            jnp.dot(whole_rows, blocks[index], preferred_element_type=jnp.float32)
            for index in range(3)
        )
    )
    return (
        query_sum.astype(jnp.bfloat16),
        key_sum.astype(jnp.bfloat16),
        value_sum.astype(jnp.bfloat16),
    )


def local(
    video,
    video_length,
    prompt,
    prompt_length,
    prompt_choice,
    ffn_gain,
    ffn_gate,
    ffn_up,
    ffn_down,
    final_gain,
    video_gain,
    w_query,
    w_key,
    w_value,
    w_text_key,
    w_text_value,
    w_out,
):
    residual = video[0].astype(jnp.float32)
    text_key, text_value, text_live = prompt_path(
        prompt,
        prompt_length,
        prompt_choice,
        ffn_gain,
        ffn_gate,
        ffn_up,
        ffn_down,
        final_gain,
        w_text_key,
        w_text_value,
    )
    query, key_rows, value_rows = video_path(residual, video_gain, w_query, w_key, w_value)
    out_full = gathered_copies(w_out, "vid", 1)
    total_rows = query.shape[0]
    text_rows = text_key.shape[0]
    width_here = query.shape[1]
    head_count = width_here // HD
    frame_length = video_length[0]
    joint_keys = jnp.concatenate([key_rows, text_key], axis=0).reshape(
        total_rows + text_rows, head_count, HD
    )
    joint_values = jnp.concatenate([value_rows, text_value], axis=0).reshape(
        total_rows + text_rows, head_count, HD
    )
    query_heads = query.reshape(total_rows, head_count, HD)
    scores = jnp.einsum(
        "qhd,khd->hqk", query_heads, joint_keys, preferred_element_type=jnp.float32
    ) * HD ** (-0.5)
    position = jnp.arange(total_rows + text_rows, dtype=jnp.int32)
    live_keys = jnp.where(
        position < total_rows, position < frame_length, position - total_rows < text_live
    )
    scores = jnp.where(live_keys[None, None, :], scores, -1e30)
    probs = jax.nn.softmax(scores, axis=-1).astype(jnp.bfloat16)
    attended = jnp.einsum("hqk,khd->qhd", probs, joint_values, preferred_element_type=jnp.float32)
    attended = attended.astype(jnp.bfloat16).reshape(total_rows, width_here)
    local_rows = video.shape[1]
    projected = lax.psum_scatter(
        jnp.dot(attended, out_full, preferred_element_type=jnp.float32).astype(jnp.bfloat16),
        "seq",
        scatter_dimension=0,
        tiled=True,
    ).astype(jnp.float32)
    row_position = lax.axis_index("seq") * local_rows + jnp.arange(local_rows, dtype=jnp.int32)
    row_live = row_position < frame_length
    updated = residual + jnp.where(row_live[:, None], projected, 0.0)
    return updated.astype(jnp.bfloat16)[None]


def solution(mesh):
    in_specs = (
        P("vid", "seq", None),
        P("vid"),
        P("vid", "seq", None),
        P(),
        P("vid"),
        P(),
        P(None, "seq"),
        P(None, "seq"),
        P("seq", None),
        P(),
        P(),
        P("vid", "seq"),
        P("vid", "seq"),
        P("vid", "seq"),
        P("vid", "seq"),
        P("vid", "seq"),
        P("seq", "vid"),
    )
    out_specs = P("vid", "seq", None)
    return jax.shard_map(local, mesh=mesh, in_specs=in_specs, out_specs=out_specs, check_vma=False)
```

profile of v0, /device:TPU:32, one launch (start us, length us, event | category | flops | bytes accessed | tf_op | source)
XLA Modules:
  0.0 484.5 jit_solution(16630161298644301142)
XLA Ops:
  6.5 0.0 copy-start
  6.5 0.0 all-gather.9.cloned.1.call-start
  6.5 1.8 pad_maximum_fusion.2
  8.4 0.0 all-gather.9.cloned.1.call-update
  8.4 0.0 all-gather.11.cloned.1.call-start
  8.5 0.9 broadcast_in_dim.85
  9.4 21.7 %all_to_all.20 = bf16[16,1,8,4096]{3,2,1,0:T(8,128)(2,1)S(1)} all-to-all(bf16[16,1,8,4096]{3,2,1,0:T(8,128)(2,1)S(1)} %broadcast_in_dim.85), channel_id=1, replica_groups=mesh['vid'=16,'seq'=16] {'seq'}, dimensions={0} | all-to-all | bytes 2097152 | tf_op jit(solution)/shard_map/all_to_all | solution.py:12
  31.1 1.0 copy-done.1
  32.1 0.3 fusion.5
  32.4 0.1 rsqrt.29
  32.5 0.0 copy-done.6
  32.5 3.0 fusion.70
  35.5 0.0 copy-done
  35.5 4.7 fusion.1
  40.2 20.2 %all_to_all.21 = bf16[16,8,4096]{2,1,0:T(8,128)(2,1)S(1)} all-to-all(bf16[16,8,4096]{2,1,0:T(8,128)(2,1)} %fusion.1), channel_id=1, replica_groups=mesh['vid'=16,'seq'=16] {'seq'}, dimensions={0} | all-to-all | bytes 2097152 | tf_op jit(solution)/shard_map/all_to_all | solution.py:34
  60.4 0.1 convert_reduce_fusion
  60.6 0.0 copy-done.4
  60.6 0.1 multiply_reduce_fusion
  60.7 0.0 copy-done.7
  60.7 0.1 fusion.76
  60.8 0.1 broadcast_in_dim.87
  60.9 20.3 %all_to_all.22 = bf16[16,8,4096]{2,1,0:T(8,128)(2,1)} all-to-all(bf16[16,8,4096]{2,1,0:T(8,128)(2,1)S(1)} %broadcast_in_dim.87), channel_id=1, replica_groups=mesh['vid'=16,'seq'=16] {'seq'}, dimensions={0} | all-to-all | bytes 2097152 | tf_op jit(solution)/shard_map/all_to_all | solution.py:12
  81.2 44.5 %all-gather.9.cloned.1.call-done = bf16[4096,512]{1,0:T(8,128)(2,1)} async-done(((bf16[256,512]{1,0:T(8,128)(2,1)}), bf16[4096,512]{1,0:T(8,128)(2,1)}) %all-gather.9.cloned.1.call-update) | async-done | bytes 4194320 | tf_op jit(solution)/shard_map/all_gather | solution.py:40
  125.7 2.4 fusion.38
  128.2 0.0 copy-done.3
  128.2 0.0 copy-start.2
  128.2 0.0 copy-start.8
  128.2 0.0 copy-start.5
  128.2 2.1 fusion.41
  130.3 0.7 pad_maximum_fusion.3
  131.0 0.0 all-gather.11.cloned.1.call-update
  131.0 0.0 all-gather.5.cloned.1.call-start
  131.0 0.0 copy-done.2
  131.0 0.2 fusion.48
  131.2 0.0 copy-done.8
  131.2 0.8 fusion.50
  132.1 0.0 all-gather.5.cloned.1.call-update
  132.1 0.0 all-gather.7.cloned.1.call-start
  132.1 0.0 copy-done.5
  132.1 1.7 pad_maximum_fusion
  133.9 0.0 all-gather.7.cloned.1.call-update
  133.9 1.0 copy.32
  134.9 1.6 broadcast_in_dim.93
  136.5 5.0 %all-to-all-start.3 = ((bf16[16,256,256]{1,2,0:T(8,128)(2,1)}), bf16[16,256,256]{1,2,0:T(8,128)(2,1)}, u32[]{:S(2)}, u32[]{:S(2)}) async-start(bf16[16,256,256]{1,2,0:T(8,128)(2,1)} %broadcast_in_dim.93), calls=%async_computation.3 | async-start | bytes 4194304 | tf_op jit(solution)/shard_map/all_to_all | solution.py:12
  141.5 0.2 reduce-scatter.2.cloned.1.call-start
  143.0 0.0 copy-done.10
  143.1 0.7 select_reduce_fusion
  143.8 0.7 fusion.81
  144.5 81.8 %all-gather.11.cloned.1.call-done = bf16[16,256,256]{2,1,0:T(8,128)(2,1)} async-done(((bf16[1,256,256]{2,1,0:T(8,128)(2,1)}), bf16[16,256,256]{2,1,0:T(8,128)(2,1)}) %all-gather.11.cloned.1.call-update) | async-done | bytes 2097168 | tf_op jit(solution)/shard_map/all_gather | solution.py:40
  226.3 1.9 fusion.44
  228.2 37.0 %all-gather.5.cloned.1.call-done = bf16[512,4096]{1,0:T(8,128)(2,1)} async-done(((bf16[32,4096]{1,0:T(8,128)(2,1)}), bf16[512,4096]{1,0:T(8,128)(2,1)}) %all-gather.5.cloned.1.call-update) | async-done | bytes 4194320 | tf_op jit(solution)/shard_map/all_gather | solution.py:96
  265.2 118.0 %all-gather.7.cloned.1.call-done = bf16[4096,768]{1,0:T(8,128)(2,1)} async-done(((bf16[256,768]{1,0:T(8,128)(2,1)}), bf16[4096,768]{1,0:T(8,128)(2,1)}) %all-gather.7.cloned.1.call-update) | async-done | bytes 6291472 | tf_op jit(solution)/shard_map/all_gather | solution.py:40
  383.2 4.1 fusion.22
  387.4 0.7 pad_maximum_fusion.1
  388.1 1.9 copy.34
  390.0 5.0 %fusion.25 = bf16[512,256]{0,1:T(8,128)(2,1)} fusion(bf16[512,4096]{1,0:T(8,128)(2,1)} %all-gather.5.cloned.1.call-done, bf16[4096,768]{1,0:T(8,128)(2,1)} %all-gather.7.cloned.1.call-done), kind=kOutput, calls=%fused_computation.31 | convolution fusion | flops 1073872896 | bytes 6553600 | tf_op jit(solution)/shard_map/dot_general | solution.py:100
  395.0 3.6 fusion.28
  398.6 2.2 fusion.91
  400.7 3.2 fusion.21
  403.9 0.0 all-to-all-done.3
  403.9 4.9 %convolution_convert_fusion = bf16[512,4096]{1,0:T(8,128)(2,1)} fusion(bf16[512,256]{0,1:T(8,128)(2,1)} %bitcast.94, bf16[256,4096]{0,1:T(8,128)(2,1)} %bitcast.17), kind=kOutput, calls=%fused_computation.1 | convolution fusion | flops 1075838976 | bytes 6553600 | tf_op jit(solution)/shard_map/dot_general | solution.py:170
  408.8 0.0 reduce-scatter.2.cloned.1.call-update
  408.9 67.3 %reduce-scatter.2.cloned.1.call-done = bf16[32,4096]{1,0:T(8,128)(2,1)} async-done(((bf16[512,4096]{1,0:T(8,128)(2,1)}), bf16[32,4096]{1,0:T(8,128)(2,1)}) %reduce-scatter.2.cloned.1.call-update) | async-done | bytes 262160 | tf_op jit(solution)/shard_map/reduce_scatter | solution.py:169
  476.2 1.8 fusion.59
  (13 shorter events, 0.1 us)
Async XLA Ops:
  6.5 29.0 %copy-start = (bf16[384,4096]{1,0:T(8,128)(2,1)S(1)}, bf16[384,4096]{1,0:T(8,128)(2,1)}, u32[]{:S(2)}) copy-start(bf16[384,4096]{1,0:T(8,128)(2,1)} %param.25) | copy-start | bytes 9437188
  6.5 25.9 %copy-start.6 = (f32[4096]{0:T(1024)S(1)}, f32[4096]{0:T(1024)}, u32[]{:S(2)}) copy-start(f32[4096]{0:T(1024)} %param.22) | copy-start | bytes 49156
  6.5 119.2 %all-gather.9.cloned.1.call-start = ((), (), s32[]{:S(2)}) async-start(), calls=%async_computation.7 | async-start | bytes 4456448 | tf_op jit(solution)/shard_map/all_gather | solution.py:40
  8.4 217.9 %all-gather.11.cloned.1.call-start = ((), (), s32[]{:S(2)}) async-start(), calls=%async_computation.8 | async-start | bytes 2228224 | tf_op jit(solution)/shard_map/all_gather | solution.py:40
  31.1 1.0 copy-start.1
  40.2 20.4 %copy-start.4 = (bf16[1,8,4096]{2,1,0:T(8,128)(2,1)S(1)}, bf16[1,8,4096]{2,1,0:T(8,128)(2,1)}, u32[]{:S(2)}) copy-start(bf16[1,8,4096]{2,1,0:T(8,128)(2,1)} %param.19) | copy-start | bytes 196612
  40.2 20.5 %copy-start.7 = (f32[4096]{0:T(1024)S(1)}, f32[4096]{0:T(1024)}, u32[]{:S(2)}) copy-start(f32[4096]{0:T(1024)} %param.26) | copy-start | bytes 49156
  125.7 2.4 copy-start.3
  128.2 2.9 copy-start.2
  128.2 3.0 copy-start.8
  128.2 3.9 copy-start.5
  131.0 134.2 %all-gather.5.cloned.1.call-start = ((), (), s32[]{:S(2)}) async-start(), calls=%async_computation.5 | async-start | bytes 4456448 | tf_op jit(solution)/shard_map/all_gather | solution.py:96
  132.1 251.2 %all-gather.7.cloned.1.call-start = ((), (), s32[]{:S(2)}) async-start(), calls=%async_computation.6 | async-start | bytes 6684672 | tf_op jit(solution)/shard_map/all_gather | solution.py:40
  136.5 6.6 %copy-start.10 = (s32[16]{0:T(128)S(1)}, s32[16]{0:T(128)}, u32[]{:S(2)}) copy-start(s32[16]{0:T(128)} %param.20) | copy-start | bytes 196
  136.5 267.4 %all-to-all-start.3 = ((bf16[16,256,256]{1,2,0:T(8,128)(2,1)}), bf16[16,256,256]{1,2,0:T(8,128)(2,1)}, u32[]{:S(2)}, u32[]{:S(2)}) async-start(bf16[16,256,256]{1,2,0:T(8,128)(2,1)} %broadcast_in_dim.93), calls=%async_computation.3 | async-start | bytes 4194304 | tf_op jit(solution)/shard_map/all_to_all | solution.py:12
  141.5 334.7 %reduce-scatter.2.cloned.1.call-start = ((), (), s32[]{:S(2)}) async-start(), calls=%async_computation.9 | async-start | bytes 4456448 | tf_op jit(solution)/shard_map/reduce_scatter | solution.py:169
  390.0 5.0 %copy-start.9 = (bf16[512,4096]{1,0:T(8,128)(2,1)S(1)}, bf16[512,4096]{1,0:T(8,128)(2,1)}, u32[]{:S(2)}) copy-start(bf16[512,4096]{1,0:T(8,128)(2,1)} %all-gather.5.cloned.1.call-done) | copy-start | bytes 12582916
Sparse Core Ops, SparseCore 0:
  9.9 115.7 all-gather.8
  131.1 95.1 all-gather.10
  228.1 37.0 all-gather.4
  267.7 115.5 all-gather.6
  409.0 67.1 reduce-scatter.1
where the time goes:
time: 485 us
  waiting for transfers between devices  349 us (72%)
  blocking collectives  62.2 us (13%)
  matrix products  35.2 us (7%)
  between operations  14.6 us (3%)
  other arithmetic  11.8 us (2%)
  local copies, waits for them, and re-layouts  6.59 us (1%)
  starting transfers between devices  5.37 us (1%)
    all_gather x3, waiting for transfers between devices, side_by_side(): lax.all_gather(both, axis, axis=dim, tiled=True)  244 us
    reduce_scatter x1, waiting for transfers between devices, local(): lax.psum_scatter(jnp.dot(attended, out_full, preferred_element_type=jnp.f...  67.3 us
    all_to_all x2, blocking collectives, sent_to_all(): lax.all_to_all(jnp.broadcast_to(x[None], (devices, *x.shape)), axis, 0, 0...  42 us
    all_gather x1, waiting for transfers between devices, video_path(): whole_rows = lax.all_gather(normed, 'seq', axis=0, tiled=True)  37 us
    all_to_all x1, blocking collectives, sent_and_summed(): lax.all_to_all(tiles, axis, split_axis=0, concat_axis=0, tiled=True)  20.2 us
    dot_general x3, matrix products, video_path(): jnp.dot(whole_rows, blocks[index], preferred_element_type=jnp.float32)  12.7 us
  transfers between devices with their start and end apart: 6, of which 5 were waited for; matrix products, arithmetic and copies ran while one was open for 8% of the time, Pallas kernels for 0%

commit v1 on v0

--- a/solution.py
+++ b/solution.py
@@ -5,6 +5,11 @@
 
 HD = 128
 epsilon = 1e-06
+
+
+def gather_over(value, axis, dim):
+    sent = jnp.stack([value] * lax.axis_size(axis))
+    return jnp.concatenate(lax.all_to_all(sent, axis, 0, 0), axis=dim)
 
 
 def sent_to_all(x, axis):
@@ -93,7 +98,7 @@
 
 def video_path(residual, video_gain, w_query, w_key, w_value):
     normed = rms_norm(residual, video_gain).astype(jnp.bfloat16)
-    whole_rows = lax.all_gather(normed, "seq", axis=0, tiled=True)
+    whole_rows = gather_over(normed, "seq", 0)
     blocks = side_by_side((w_query, w_key, w_value), "vid", 0, 1)
     query_sum, key_sum, value_sum = tuple(
         (

time: 485 us -> 479 us (0.988)
  waiting for transfers between devices: 349 us -> 334 us
  starting transfers between devices: 5.37 us -> 11.4 us
    all_to_all x0 -> x1, waiting for transfers between devices: none -> 51.2 us  [gather_over(): return jnp.concatenate(lax.all_to_all(sent, axis, 0, 0), axis=dim)]
    all_gather x1 -> x0, waiting for transfers between devices: 37 us -> none  [video_path(): whole_rows = lax.all_gather(normed, 'seq', axis=0, tiled=True)]
    all_gather x3, waiting for transfers between devices: 244 us -> 215 us  [side_by_side(): lax.all_gather(both, axis, axis=dim, tiled=True)]
  transfers between devices with their start and end apart: 6 -> 6, of which waited for: 5 -> 5; matrix products, arithmetic and copies ran while one was open for 8% -> 9% of each run, Pallas kernels for 0% -> 0%
where the time goes in v1:
time: 479 us
  waiting for transfers between devices  334 us (70%)
  blocking collectives  62.2 us (13%)
  matrix products  36.3 us (8%)
  between operations  14.6 us (3%)
  starting transfers between devices  11.4 us (2%)
  other arithmetic  10.9 us (2%)
  local copies, waits for them, and re-layouts  9.18 us (2%)
    all_gather x3, waiting for transfers between devices, side_by_side(): lax.all_gather(both, axis, axis=dim, tiled=True)  215 us
    reduce_scatter x1, waiting for transfers between devices, local(): lax.psum_scatter(jnp.dot(attended, out_full, preferred_element_type=jnp.f...  67.4 us
    all_to_all x1, waiting for transfers between devices, gather_over(): return jnp.concatenate(lax.all_to_all(sent, axis, 0, 0), axis=dim)  51.2 us
    all_to_all x2, blocking collectives, sent_to_all(): lax.all_to_all(jnp.broadcast_to(x[None], (devices, *x.shape)), axis, 0, 0...  42 us
    all_to_all x1, blocking collectives, sent_and_summed(): lax.all_to_all(tiles, axis, split_axis=0, concat_axis=0, tiled=True)  20.2 us
    dot_general x3, matrix products, video_path(): jnp.dot(whole_rows, blocks[index], preferred_element_type=jnp.float32)  13.8 us
  transfers between devices with their start and end apart: 6, of which 5 were waited for; matrix products, arithmetic and copies ran while one was open for 9% of the time, Pallas kernels for 0%

profile of v1, /device:TPU:32, one launch (start us, length us, event | category | flops | bytes accessed | tf_op | source)
XLA Modules:
  0.0 478.5 jit_solution(7748374212029672043)
XLA Ops:
  6.5 0.0 copy-start
  6.5 0.0 all-gather.6.cloned.1.call-start
  6.5 1.8 pad_maximum_fusion.2
  8.4 0.0 all-gather.6.cloned.1.call-update
  8.4 0.0 all-gather.8.cloned.1.call-start
  8.5 0.9 broadcast_in_dim.85
  9.4 21.7 %all_to_all.25 = bf16[16,1,8,4096]{3,2,1,0:T(8,128)(2,1)S(1)} all-to-all(bf16[16,1,8,4096]{3,2,1,0:T(8,128)(2,1)S(1)} %broadcast_in_dim.85), channel_id=1, replica_groups=mesh['vid'=16,'seq'=16] {'seq'}, dimensions={0} | all-to-all | bytes 2097152 | tf_op jit(solution)/shard_map/all_to_all | solution.py:17
  31.1 1.0 copy-done.1
  32.1 0.3 fusion.5
  32.4 0.1 rsqrt.29
  32.5 0.0 copy-done.6
  32.5 3.0 fusion.73
  35.5 0.0 copy-done
  35.5 4.7 fusion.1
  40.2 20.2 %all_to_all.26 = bf16[16,8,4096]{2,1,0:T(8,128)(2,1)S(1)} all-to-all(bf16[16,8,4096]{2,1,0:T(8,128)(2,1)} %fusion.1), channel_id=1, replica_groups=mesh['vid'=16,'seq'=16] {'seq'}, dimensions={0} | all-to-all | bytes 2097152 | tf_op jit(solution)/shard_map/all_to_all | solution.py:39
  60.4 0.1 convert_reduce_fusion
  60.6 0.0 copy-done.4
  60.6 0.1 multiply_reduce_fusion
  60.7 0.0 copy-done.7
  60.7 0.1 fusion.79
  60.8 0.1 broadcast_in_dim.87
  60.9 20.3 %all_to_all.27 = bf16[16,8,4096]{2,1,0:T(8,128)(2,1)} all-to-all(bf16[16,8,4096]{2,1,0:T(8,128)(2,1)S(1)} %broadcast_in_dim.87), channel_id=1, replica_groups=mesh['vid'=16,'seq'=16] {'seq'}, dimensions={0} | all-to-all | bytes 2097152 | tf_op jit(solution)/shard_map/all_to_all | solution.py:17
  81.2 44.5 %all-gather.6.cloned.1.call-done = bf16[4096,512]{1,0:T(8,128)(2,1)} async-done(((bf16[256,512]{1,0:T(8,128)(2,1)}), bf16[4096,512]{1,0:T(8,128)(2,1)}) %all-gather.6.cloned.1.call-update) | async-done | bytes 4194320 | tf_op jit(solution)/shard_map/all_gather | solution.py:45
  125.7 2.4 fusion.38
  128.2 0.0 copy-done.3
  128.2 0.0 copy-start.5
  128.2 0.0 copy-start.2
  128.2 0.0 copy-start.8
  128.2 2.1 fusion.41
  130.3 0.7 pad_maximum_fusion.3
  131.0 0.0 all-gather.8.cloned.1.call-update
  131.0 0.0 all-gather.4.cloned.1.call-start
  131.0 0.0 copy-done.5
  131.0 1.7 pad_maximum_fusion
  132.8 0.0 all-gather.4.cloned.1.call-update
  132.8 0.0 copy-done.2
  132.8 0.2 fusion.50
  133.0 0.0 copy-done.8
  133.0 0.1 fusion.61
  133.1 2.6 stack.5
  135.7 4.5 all-to-all-start
  140.3 1.0 copy.32
  141.3 51.2 %all-to-all-done = bf16[16,32,4096]{2,1,0:T(8,128)(2,1)} async-done(((bf16[16,32,4096]{2,1,0:T(8,128)(2,1)}), bf16[16,32,4096]{2,1,0:T(8,128)(2,1)}, u32[]{:S(2)}, u32[]{:S(2)}) %all-to-all-start) | async-done | bytes 4194336 | tf_op jit(solution)/shard_map/all_to_all | solution.py:12
  192.5 1.6 broadcast_in_dim.93
  194.0 6.5 %all-to-all-start.4 = ((bf16[16,256,256]{1,2,0:T(8,128)(2,1)}), bf16[16,256,256]{1,2,0:T(8,128)(2,1)}, u32[]{:S(2)}, u32[]{:S(2)}) async-start(bf16[16,256,256]{1,2,0:T(8,128)(2,1)} %broadcast_in_dim.93), calls=%async_computation.4 | async-start | bytes 4194304 | tf_op jit(solution)/shard_map/all_to_all | solution.py:17
  200.6 0.2 reduce-scatter.2.cloned.1.call-start
  202.1 0.0 copy-done.9
  202.1 0.6 select_reduce_fusion
  202.8 0.6 fusion.84
  203.4 51.4 %all-gather.8.cloned.1.call-done = bf16[16,256,256]{2,1,0:T(8,128)(2,1)} async-done(((bf16[1,256,256]{2,1,0:T(8,128)(2,1)}), bf16[16,256,256]{2,1,0:T(8,128)(2,1)}) %all-gather.8.cloned.1.call-update) | async-done | bytes 2097168 | tf_op jit(solution)/shard_map/all_gather | solution.py:45
  254.8 1.9 fusion.44
  256.7 119.3 %all-gather.4.cloned.1.call-done = bf16[4096,768]{1,0:T(8,128)(2,1)} async-done(((bf16[256,768]{1,0:T(8,128)(2,1)}), bf16[4096,768]{1,0:T(8,128)(2,1)}) %all-gather.4.cloned.1.call-update) | async-done | bytes 6291472 | tf_op jit(solution)/shard_map/all_gather | solution.py:45
  376.1 4.1 fusion.22
  380.2 0.7 pad_maximum_fusion.1
  380.9 1.9 copy.34
  382.8 4.9 %fusion.25 = bf16[512,256]{0,1:T(8,128)(2,1)} fusion(bf16[512,4096]{1,0:T(8,128)(2,1)} %bitcast.3, bf16[4096,768]{1,0:T(8,128)(2,1)} %all-gather.4.cloned.1.call-done), kind=kOutput, calls=%fused_computation.31 | convolution fusion | flops 1073872896 | bytes 6553600 | tf_op jit(solution)/shard_map/dot_general | solution.py:105
  387.7 4.8 %fusion.28 = bf16[512,256]{1,0:T(8,128)(2,1)} fusion(bf16[512,4096]{1,0:T(8,128)(2,1)} %bitcast.3, bf16[4096,768]{1,0:T(8,128)(2,1)} %all-gather.4.cloned.1.call-done), kind=kOutput, calls=%fused_computation.32 | convolution fusion | flops 1073872896 | bytes 6553600 | tf_op jit(solution)/shard_map/dot_general | solution.py:105
  392.5 2.2 fusion.94
  394.6 3.2 fusion.21
  397.8 0.0 all-to-all-done.4
  397.8 4.9 %convolution_convert_fusion = bf16[512,4096]{1,0:T(8,128)(2,1)} fusion(bf16[512,256]{0,1:T(8,128)(2,1)} %bitcast.104, bf16[256,4096]{0,1:T(8,128)(2,1)} %bitcast.18), kind=kOutput, calls=%fused_computation.1 | convolution fusion | flops 1075838976 | bytes 6553600 | tf_op jit(solution)/shard_map/dot_general | solution.py:175
  402.8 0.0 reduce-scatter.2.cloned.1.call-update
  402.8 67.4 %reduce-scatter.2.cloned.1.call-done = bf16[32,4096]{1,0:T(8,128)(2,1)} async-done(((bf16[512,4096]{1,0:T(8,128)(2,1)}), bf16[32,4096]{1,0:T(8,128)(2,1)}) %reduce-scatter.2.cloned.1.call-update) | async-done | bytes 262160 | tf_op jit(solution)/shard_map/reduce_scatter | solution.py:174
  470.2 1.8 fusion.62
  (11 shorter events, 0.0 us)
Async XLA Ops:
  6.5 29.0 %copy-start = (bf16[384,4096]{1,0:T(8,128)(2,1)S(1)}, bf16[384,4096]{1,0:T(8,128)(2,1)}, u32[]{:S(2)}) copy-start(bf16[384,4096]{1,0:T(8,128)(2,1)} %param.25) | copy-start | bytes 9437188
  6.5 25.9 %copy-start.6 = (f32[4096]{0:T(1024)S(1)}, f32[4096]{0:T(1024)}, u32[]{:S(2)}) copy-start(f32[4096]{0:T(1024)} %param.22) | copy-start | bytes 49156
  6.5 119.2 %all-gather.6.cloned.1.call-start = ((), (), s32[]{:S(2)}) async-start(), calls=%async_computation.7 | async-start | bytes 4456448 | tf_op jit(solution)/shard_map/all_gather | solution.py:45
  8.4 246.4 %all-gather.8.cloned.1.call-start = ((), (), s32[]{:S(2)}) async-start(), calls=%async_computation.8 | async-start | bytes 2228224 | tf_op jit(solution)/shard_map/all_gather | solution.py:45
  31.1 1.0 copy-start.1
  40.2 20.4 %copy-start.4 = (bf16[1,8,4096]{2,1,0:T(8,128)(2,1)S(1)}, bf16[1,8,4096]{2,1,0:T(8,128)(2,1)}, u32[]{:S(2)}) copy-start(bf16[1,8,4096]{2,1,0:T(8,128)(2,1)} %param.19) | copy-start | bytes 196612
  40.2 20.5 %copy-start.7 = (f32[4096]{0:T(1024)S(1)}, f32[4096]{0:T(1024)}, u32[]{:S(2)}) copy-start(f32[4096]{0:T(1024)} %param.26) | copy-start | bytes 49156
  125.7 2.4 copy-start.3
  128.2 2.9 copy-start.5
  128.2 4.6 copy-start.2
  128.2 4.8 %copy-start.8 = (f32[4096]{0:T(1024)S(1)}, f32[4096]{0:T(1024)}, u32[]{:S(2)}) copy-start(f32[4096]{0:T(1024)} %param.27) | copy-start | bytes 49156
  131.0 245.1 %all-gather.4.cloned.1.call-start = ((), (), s32[]{:S(2)}) async-start(), calls=%async_computation.6 | async-start | bytes 6684672 | tf_op jit(solution)/shard_map/all_gather | solution.py:45
  135.7 56.7 %all-to-all-start = ((bf16[16,32,4096]{2,1,0:T(8,128)(2,1)}), bf16[16,32,4096]{2,1,0:T(8,128)(2,1)}, u32[]{:S(2)}, u32[]{:S(2)}) async-start(bf16[16,32,4096]{2,1,0:T(8,128)(2,1)} %stack.5), calls=%async_computation | async-start | bytes 8388608 | tf_op jit(solution)/shard_map/all_to_all | solution.py:12
  194.0 8.1 %copy-start.9 = (s32[16]{0:T(128)S(1)}, s32[16]{0:T(128)}, u32[]{:S(2)}) copy-start(s32[16]{0:T(128)} %param.20) | copy-start | bytes 196
  194.0 203.8 %all-to-all-start.4 = ((bf16[16,256,256]{1,2,0:T(8,128)(2,1)}), bf16[16,256,256]{1,2,0:T(8,128)(2,1)}, u32[]{:S(2)}, u32[]{:S(2)}) async-start(bf16[16,256,256]{1,2,0:T(8,128)(2,1)} %broadcast_in_dim.93), calls=%async_computation.4 | async-start | bytes 4194304 | tf_op jit(solution)/shard_map/all_to_all | solution.py:17
  200.6 269.6 %reduce-scatter.2.cloned.1.call-start = ((), (), s32[]{:S(2)}) async-start(), calls=%async_computation.9 | async-start | bytes 4456448 | tf_op jit(solution)/shard_map/reduce_scatter | solution.py:174
Sparse Core Ops, SparseCore 0:
  9.9 115.7 all-gather.5
  131.1 123.6 all-gather.7
  257.4 118.6 all-gather.3
  402.9 67.2 reduce-scatter.1
